TPU v7x, 128 devices: a whole 4x4x4 slice. The times are simulated.
128 devices in a mesh: dp: 4 (over y_lo, core), seq: 32 (over x, y_hi, z).
Axes of the slice: x: 4, y: 4 (y_hi: 2, y_lo: 2; y = y_hi * 2 + y_lo), z: 4, core: 2. Of those that a mesh axis runs over, the one named last changes fastest.
Arguments:
- siblings: int32 [4, 64, 16], P('dp', 'seq'), may hold values from 0 to 63, all different within a row
- queries: bfloat16 [4, 64, 512, 2560], P('dp', 'seq'), may hold values from -6 to 6
- grad_out: bfloat16 [4, 64, 512, 2560], P('dp', 'seq'), may hold values from -6 to 6
- keys_in: bfloat16 [4, 64, 16, 512], P('dp', 'seq'), may hold values from -4 to 4
- input_values: bfloat16 [4, 64, 16, 512], P('dp', 'seq'), may hold values from -6 to 6
- summary: bfloat16 [4, 64, 16, 5120], P('dp', 'seq'), may hold values from -6 to 6
Outputs:
- query_gradient: bfloat16 [4, 64, 512, 2560], P('dp', 'seq')
- kv_weight_grad: float32 [5120, 1024], P(('dp', 'seq'))
Inputs may be any that keep to these rules, and one draw needn't show every extreme that they name: `siblings`: the 16 entries of one completion's list are distinct completions of the same prompt.
All inputs are finite; a program needn't handle non-finite values.
Results may differ from a plain program's by a relative error of at most 0.012.
Values may be sent and summed in bfloat16 or wider, within the bound.
A program may use at most 192 MiB of HBM per device.

v0:
```python
import math
import jax
import jax.numpy as jnp
from jax import lax
from jax.sharding import PartitionSpec as P

HEAD_SIZE = 128


def group_grads(query_tile_block, incoming_gradient, key_tile_block, value_tile_block, scaling):
    scores = (
        jnp.einsum(
            "ctrd,cld->crtl", query_tile_block, key_tile_block, preferred_element_type=jnp.float32
        )
        * scaling
    )
    largest = jnp.max(scores, axis=-1, keepdims=True)
    exponent = jnp.exp(scores - largest)
    probability = exponent / jnp.sum(exponent, axis=-1, keepdims=True)
    prob_half = probability.astype(jnp.bfloat16)
    attended = jnp.einsum(
        "crtl,cld->ctrd", prob_half, value_tile_block, preferred_element_type=jnp.float32
    )
    token_delta = jnp.sum(incoming_gradient * attended, axis=-1)
    row_delta = jnp.transpose(token_delta, (0, 2, 1))[..., None]
    prob_grad = jnp.einsum(
        "ctrd,cld->crtl", incoming_gradient, value_tile_block, preferred_element_type=jnp.float32
    )
    score_half = (probability * (prob_grad - row_delta)).astype(jnp.bfloat16)
    query_gradient = (
        jnp.einsum("crtl,cld->ctrd", score_half, key_tile_block, preferred_element_type=jnp.float32)
        * scaling
    )
    key_gradient = (
        jnp.einsum(
            "crtl,ctrd->cld", score_half, query_tile_block, preferred_element_type=jnp.float32
        )
        * scaling
    )
    value_gradient = jnp.einsum(
        "crtl,ctrd->cld", prob_half, incoming_gradient, preferred_element_type=jnp.float32
    )
    return (query_gradient, key_gradient, value_gradient)


def per_device(siblings, queries, grad_out, keys_in, input_values, summary):
    keys_all, values_all = (
        lax.all_gather(keys_in, "seq", axis=1, tiled=True),
        lax.all_gather(input_values, "seq", axis=1, tiled=True),
    )
    sibling = siblings[0]
    own_count, row_length = (queries.shape[1], queries.shape[2])
    everyone = keys_all.shape[1]
    neighbours, positions, key_value_width = (sibling.shape[1], keys_in.shape[2], keys_in.shape[3])
    kv_heads = key_value_width // HEAD_SIZE
    group_span = queries.shape[3] // kv_heads
    group_size = group_span // HEAD_SIZE
    scaling = 1.0 / math.sqrt(HEAD_SIZE)
    key_rows = keys_all[0][sibling].reshape(own_count, neighbours * positions, key_value_width)
    value_rows = values_all[0][sibling].reshape(own_count, neighbours * positions, key_value_width)
    query_parts, key_parts, value_parts = ([], [], [])
    for kv_head in range(kv_heads):
        query_tile_block = queries[
            0, :, :, kv_head * group_span : (kv_head + 1) * group_span
        ].reshape(own_count, row_length, group_size, HEAD_SIZE)
        incoming_gradient = grad_out[
            0, :, :, kv_head * group_span : (kv_head + 1) * group_span
        ].reshape(own_count, row_length, group_size, HEAD_SIZE)
        key_tile_block = key_rows[:, :, kv_head * HEAD_SIZE : (kv_head + 1) * HEAD_SIZE]
        value_tile_block = value_rows[:, :, kv_head * HEAD_SIZE : (kv_head + 1) * HEAD_SIZE]
        query_gradient, key_gradient, value_gradient = group_grads(
            query_tile_block, incoming_gradient, key_tile_block, value_tile_block, scaling
        )
        query_parts.append(query_gradient.reshape(own_count, row_length, group_span))
        key_parts.append(key_gradient)
        value_parts.append(value_gradient)
    query_out = jnp.concatenate(query_parts, axis=-1).astype(jnp.bfloat16)
    key_gradient = jnp.concatenate(key_parts, axis=-1).reshape(
        own_count * neighbours, positions * key_value_width
    )
    value_gradient = jnp.concatenate(value_parts, axis=-1).reshape(
        own_count * neighbours, positions * key_value_width
    )
    targets = sibling.reshape(-1)
    placing = (targets[:, None] == jnp.arange(everyone, dtype=jnp.int32)[None, :]).astype(
        jnp.float32
    )
    key_buffer = jnp.dot(placing.T, key_gradient, precision=lax.Precision.HIGHEST)
    value_buffer = jnp.dot(placing.T, value_gradient, precision=lax.Precision.HIGHEST)
    owner_keys, owner_values = (
        lax.psum_scatter(key_buffer, "seq", scatter_dimension=0, tiled=True),
        lax.psum_scatter(value_buffer, "seq", scatter_dimension=0, tiled=True),
    )
    grads_half = jnp.concatenate(
        [
            owner_keys.astype(jnp.bfloat16).reshape(own_count * positions, key_value_width),
            owner_values.astype(jnp.bfloat16).reshape(own_count * positions, key_value_width),
        ],
        axis=1,
    )
    hidden = summary[0].reshape(own_count * positions, summary.shape[3])
    weight_grad = lax.psum_scatter(
        jnp.einsum("sd,sk->dk", hidden, grads_half, preferred_element_type=jnp.float32),
        ("dp", "seq"),
        scatter_dimension=0,
        tiled=True,
    )
    return (query_out[None], weight_grad)


def solution(mesh):
    placed = (
        P("dp", "seq", None),
        P("dp", "seq", None, None),
        P("dp", "seq", None, None),
        P("dp", "seq", None, None),
        P("dp", "seq", None, None),
        P("dp", "seq", None, None),
    )
    return jax.shard_map(
        per_device,
        mesh=mesh,
        in_specs=placed,
        out_specs=(P("dp", "seq", None, None), P(("dp", "seq"), None)),
        check_vma=False,
    )
```

profile of v0, /device:TPU:1, one launch (start us, length us, event | category | flops | bytes accessed | tf_op | source)
XLA Modules:
  0.0 1172.4 jit_solution(1729174952819636855)
XLA Ops:
  10.2 4.6 fusion.72
  22.7 4.6 fusion.73
  35.6 43.3 %all-gather.5.cloned.1.call-done = bf16[1,64,16,512]{3,2,0,1:T(8,128)(2,1)} async-done(((bf16[1,2,16,512]{3,2,0,1:T(8,128)(2,1)}), bf16[1,64,16,512]{3,2,0,1:T(8,128)(2,1)}) %all-gather.5.cloned.1.call-update) | async-done | bytes 1048592 | tf_op jit(solution)/shard_map/all_gather | solution.py:49
  79.0 2.6 gather_fusion.1
  81.6 63.8 %all-gather.3.cloned.1.call-done = bf16[1,64,16,512]{3,2,0,1:T(8,128)(2,1)} async-done(((bf16[1,2,16,512]{3,2,0,1:T(8,128)(2,1)}), bf16[1,64,16,512]{3,2,0,1:T(8,128)(2,1)}) %all-gather.3.cloned.1.call-update) | async-done | bytes 1048592 | tf_op jit(solution)/shard_map/all_gather | solution.py:48
  147.2 5.6 fusion.74
  152.8 3.3 fusion.43
  159.9 5.4 fusion.76
  165.3 3.3 fusion.41
  172.5 5.4 fusion.75
  177.9 3.2 fusion.42
  185.0 5.4 fusion.77
  190.3 3.5 fusion.40
  195.8 3.5 fusion.5
  210.9 3.5 fusion.17
  223.3 186.3 %all-reduce.4 = (bf16[64,8192]{1,0:T(8,128)(2,1)S(1)}, bf16[64,8192]{1,0:T(8,128)(2,1)}) all-reduce(f32[64,8192]{1,0:T(8,128)} %fusion.63, f32[64,8192]{1,0:T(8,128)S(1)} %fusion.64), channel_id=3, replica_groups=mesh['dp'=4,'seq'=32] {'seq'}, use_global_device_ids=true, to_apply=%region_13.0.clone | all-reduce | flops 1048576 | bytes 6291456
  410.7 8.6 convolution_bitcast_fusion
  419.3 21.3 %copy.209 = f32[5120,1024]{1,0:T(8,128)} copy(f32[5120,1024]{0,1:T(8,128)} %convolution_bitcast_fusion) | data formatting | bytes 41943040
  444.1 2.6 copy.133
  448.4 2.6 copy.131
  452.6 2.6 copy.132
  456.8 2.6 copy.130
  459.5 4.6 pad_maximum_fusion
  464.0 701.8 %reduce-scatter.4.cloned.1.call-done = f32[40,1024]{1,0:T(8,128)} async-done(((f32[5120,1024]{1,0:T(8,128)}), f32[40,1024]{1,0:T(8,128)}) %reduce-scatter.4.cloned.1.call-update) | async-done | bytes 163856
  (135 shorter events, 63.4 us)
Async XLA Ops:
  7.2 403.5 %copy-start = (bf16[1,2,16,5120]{3,2,1,0:T(8,128)(2,1)S(1)}, bf16[1,2,16,5120]{3,2,1,0:T(8,128)(2,1)}, u32[]{:S(2)}) copy-start(bf16[1,2,16,5120]{3,2,1,0:T(8,128)(2,1)} %param.11) | copy-start | bytes 983044
  7.2 71.8 %all-gather.5.cloned.1.call-start = ((), (), s32[]{:S(2)}) async-start(), calls=%async_computation.2 | async-start | bytes 1081344 | tf_op jit(solution)/shard_map/all_gather | solution.py:49
  7.9 137.4 %all-gather.3.cloned.1.call-start = ((), (), s32[]{:S(2)}) async-start(), calls=%async_computation.1 | async-start | bytes 1081344 | tf_op jit(solution)/shard_map/all_gather | solution.py:48
  8.7 1157.2 %reduce-scatter.4.cloned.1.call-start = ((), (), s32[]{:S(2)}) async-start(), calls=%async_computation.3 | async-start | bytes 21135360
  29.5 4.9 copy-start.37
  147.2 37.8 %copy-start.19 = (bf16[32,16,512]{2,1,0:T(8,128)(2,1)}, bf16[32,16,512]{2,1,0:T(8,128)(2,1)S(1)}, u32[]{:S(2)}) copy-start(bf16[32,16,512]{2,1,0:T(8,128)(2,1)S(1)} %gather_fusion) | copy-start | bytes 1572868
  152.8 3.3 copy-start.28
  152.8 3.4 copy-start.3
  165.3 3.3 copy-start.30
  165.3 3.4 copy-start.1
  177.9 3.3 copy-start.32
  190.3 3.5 copy-start.21
  194.5 6.6 slice-start
  195.8 3.6 copy-start.18
  195.8 5.3 slice-start.1
  195.8 5.3 copy-start.31
  195.8 5.3 copy-start.35
  199.4 3.2 copy-start.5
  199.4 5.6 slice-start.2
  201.7 3.3 slice-start.3
  210.9 5.0 copy-start.15
  452.6 2.6 copy-start.12
  456.8 2.6 copy-start.13
  456.8 2.6 copy-start.14
  (21 other events, 35.3 us)
Sparse Core Ops, SparseCore 0:
  11.0 67.9 all-gather.4
  81.9 63.3 all-gather.2
  440.8 725.0 reduce-scatter.3
where the time goes:
time: 1170 us
  waiting for transfers between devices  810 us (69%)
  blocking collectives  186 us (16%)
  local copies, waits for them, and re-layouts  72.6 us (6%)
  matrix products  69.4 us (6%)
  other arithmetic  18.8 us (2%)
  between operations  14.8 us (1%)
    unnamed x4, waiting for transfers between devices  703 us
    unnamed x1, blocking collectives  186 us
    all_gather x1, waiting for transfers between devices, per_device(): lax.all_gather(keys_in, 'seq', axis=1, tiled=True)  63.8 us
    all_gather x1, waiting for transfers between devices, per_device(): lax.all_gather(input_values, 'seq', axis=1, tiled=True)  43.3 us
    unnamed x94, local copies, waits for them, and re-layouts  42.5 us
  transfers between devices with their start and end apart: 3, of which 3 were waited for; matrix products, arithmetic and copies ran while one was open for 4% of the time, Pallas kernels for 0%

commit v1 on v0

--- a/solution.py
+++ b/solution.py
@@ -1,3 +1,4 @@
+import functools
 import math
 import jax
 import jax.numpy as jnp
@@ -5,6 +6,15 @@
 from jax.sharding import PartitionSpec as P
 
 HEAD_SIZE = 128
+
+
+def loads_report(unit, out_dim):
+    return jnp.concatenate(
+        lax.all_to_all(jnp.stack([unit] * lax.axis_size("seq"), 0), "seq", 0, 0), out_dim
+    )
+
+
+put_slot = functools.partial(loads_report, out_dim=1)
 
 
 def group_grads(query_tile_block, incoming_gradient, key_tile_block, value_tile_block, scaling):
@@ -45,7 +55,7 @@
 
 def per_device(siblings, queries, grad_out, keys_in, input_values, summary):
     keys_all, values_all = (
-        lax.all_gather(keys_in, "seq", axis=1, tiled=True),
+        put_slot(keys_in),
         lax.all_gather(input_values, "seq", axis=1, tiled=True),
     )
     sibling = siblings[0]

time: 1170 us -> 1080 us (0.923)
  waiting for transfers between devices: 810 us -> 700 us
  local copies, waits for them, and re-layouts: 72.6 us -> 84.3 us
    all_gather x1 -> x0, waiting for transfers between devices: 63.8 us -> none  [per_device(): lax.all_gather(keys_in, 'seq', axis=1, tiled=True)]
    all_gather x1, waiting for transfers between devices: 43.3 us -> 0.01 us  [per_device(): lax.all_gather(input_values, 'seq', axis=1, tiled=True)]
    unnamed x94 -> x102, local copies, waits for them, and re-layouts: 42.5 us -> 46 us
    unnamed x4 -> x3, waiting for transfers between devices: 703 us -> 700 us
  transfers between devices with their start and end apart: 3 -> 3, of which waited for: 3 -> 1; matrix products, arithmetic and copies ran while one was open for 4% -> 9% of each run, Pallas kernels for 0% -> 0%
where the time goes in v1:
time: 1080 us
  waiting for transfers between devices  700 us (65%)
  blocking collectives  191 us (18%)
  local copies, waits for them, and re-layouts  84.3 us (8%)
  matrix products  66 us (6%)
  between operations  15.2 us (1%)
  other arithmetic  15.1 us (1%)
  starting transfers between devices  11.6 us (1%)
    unnamed x3, waiting for transfers between devices  700 us
    unnamed x1, blocking collectives  191 us
    unnamed x102, local copies, waits for them, and re-layouts  46 us
  transfers between devices with their start and end apart: 3, of which 1 were waited for; matrix products, arithmetic and copies ran while one was open for 9% of the time, Pallas kernels for 0%

profile of v1, /device:TPU:1, one launch (start us, length us, event | category | flops | bytes accessed | tf_op | source)
XLA Modules:
  0.0 1083.5 jit_solution(11455079794841888638)
XLA Ops:
  9.8 11.5 %all-to-all-start = ((bf16[32,1,2,16,512]{4,3,2,1,0:T(8,128)(2,1)}), bf16[32,1,2,16,512]{4,3,2,1,0:T(8,128)(2,1)}, u32[]{:S(2)}, u32[]{:S(2)}) async-start(bf16[32,1,2,16,512]{4,3,2,1,0:T(8,128)(2,1)} %stack.2), calls=%async_computation | async-start | bytes 2097152 | tf_op jit(solution)/shard_map/all_to_all | solution.py:13
  21.5 4.6 fusion.72
  33.9 4.6 fusion.73
  49.5 6.1 fusion.74
  55.6 4.1 fusion.76
  59.7 4.1 fusion.75
  63.7 3.4 fusion.43
  75.9 6.0 fusion.77
  81.9 3.3 fusion.40
  88.9 2.5 copy.142
  93.8 3.9 fusion.63
  97.6 2.6 gather_fusion.1
  108.9 3.5 fusion.5
  123.3 2.5 copy.137
  128.2 3.6 fusion.64
  131.8 190.8 %all-reduce.4 = (bf16[64,8192]{1,0:T(8,128)(2,1)}, bf16[64,8192]{1,0:T(8,128)(2,1)}) all-reduce(f32[64,8192]{1,0:T(8,128)} %fusion.63, f32[64,8192]{1,0:T(8,128)} %fusion.64), channel_id=3, replica_groups=mesh['dp'=4,'seq'=32] {'seq'}, use_global_device_ids=true, to_apply=%region_13.0.clone | all-reduce | flops 1048576 | bytes 6291456
  325.1 8.7 convolution_bitcast_fusion
  333.8 21.3 %copy.208 = f32[5120,1024]{1,0:T(8,128)} copy(f32[5120,1024]{0,1:T(8,128)} %convolution_bitcast_fusion) | data formatting | bytes 41943040
  356.8 2.6 copy.132
  361.1 2.6 copy.130
  365.3 2.6 copy.131
  369.6 2.6 copy.129
  372.2 4.6 pad_maximum_fusion
  376.8 699.8 %reduce-scatter.4.cloned.1.call-done = f32[40,1024]{1,0:T(8,128)} async-done(((f32[5120,1024]{1,0:T(8,128)}), f32[40,1024]{1,0:T(8,128)}) %reduce-scatter.4.cloned.1.call-update) | async-done | bytes 163856
  (145 shorter events, 66.2 us)
Async XLA Ops:
  7.2 317.9 %copy-start = (bf16[1,2,16,5120]{3,2,1,0:T(8,128)(2,1)S(1)}, bf16[1,2,16,5120]{3,2,1,0:T(8,128)(2,1)}, u32[]{:S(2)}) copy-start(bf16[1,2,16,5120]{3,2,1,0:T(8,128)(2,1)} %param.11) | copy-start | bytes 983044
  7.2 14.2 %copy-start.36 = (s32[1,2,16]{2,1,0:T(2,128)S(1)}, s32[1,2,16]{2,1,0:T(2,128)}, u32[]{:S(2)}) copy-start(s32[1,2,16]{2,1,0:T(2,128)} %param.6) | copy-start | bytes 388
  7.2 90.5 %all-gather.2.cloned.1.call-start = ((), (), s32[]{:S(2)}) async-start(), calls=%async_computation.2 | async-start | bytes 1081344 | tf_op jit(solution)/shard_map/all_gather | solution.py:59
  9.8 37.8 %all-to-all-start = ((bf16[32,1,2,16,512]{4,3,2,1,0:T(8,128)(2,1)}), bf16[32,1,2,16,512]{4,3,2,1,0:T(8,128)(2,1)}, u32[]{:S(2)}, u32[]{:S(2)}) async-start(bf16[32,1,2,16,512]{4,3,2,1,0:T(8,128)(2,1)} %stack.2), calls=%async_computation | async-start | bytes 2097152 | tf_op jit(solution)/shard_map/all_to_all | solution.py:13
  21.3 1055.3 %reduce-scatter.4.cloned.1.call-start = ((), (), s32[]{:S(2)}) async-start(), calls=%async_computation.3 | async-start | bytes 21135360
  43.4 3.0 copy-start.37
  49.5 6.1 copy-start.26
  55.6 4.1 copy-start.24
  63.7 3.4 copy-start.13
  63.7 5.1 copy-start.29
  67.2 4.7 slice-start
  68.9 3.0 slice-start.1
  69.7 3.0 copy-start.1
  81.9 4.9 copy-start.7
  105.0 3.8 copy-start.30
  105.0 3.8 copy-start.35
  107.2 6.2 slice-start.4
  108.8 3.6 copy-start.28
  108.9 4.6 slice-start.5
  112.4 3.6 slice-start.2
  115.0 4.3 slice-start.6
  116.0 3.3 slice-start.7
  369.6 2.6 copy-start.21
  369.6 2.6 copy-start.22
  (25 other events, 50.4 us)
Sparse Core Ops, SparseCore 0:
  11.0 71.9 all-gather.1
  355.2 721.3 reduce-scatter.3
